TPU v7x, 128 devices: a whole 4x4x4 slice. The times are simulated.
128 devices in a mesh: section: 16 (over z, y_lo, core), tensor: 8 (over y_hi, x).
Axes of the slice: x: 4, y: 4 (y_hi: 2, y_lo: 2; y = y_hi * 2 + y_lo), z: 4, core: 2. Of those that a mesh axis runs over, the one named last changes fastest.
Arguments:
- token_ids: int32 [4096], P('section'), may hold values from 0 to 152063, as said below
- column_order: int32 [8192], replicated, may hold values from 0 to 8191, each once
- residual: bfloat16 [4096, 8192], P('section', 'tensor'), may hold values from -40 to 40
- attn_out: bfloat16 [4096, 8192], P('section', 'tensor'), may hold values from -6 to 6
- out_proj: bfloat16 [8192, 8192], P(None, 'tensor'), may hold values from -0.0625 to 0.0625
- norm_gain: float32 [8192], P('tensor'), may hold values from 0.5 to 1.5
Outputs:
- factored: float32 [8192, 8192], P('section', 'tensor')
Inputs may be any that keep to these rules, and one draw needn't show every extreme that they name: `token_ids`: id 0 marks padding. In each block of 256 tokens of one section index the padding fills trailing positions, and each block holds at least one non-padding token.
All inputs are finite; a program needn't handle non-finite values.
Results may differ from a plain program's by a relative error of at most 0.0067.
Values may be sent and summed in bfloat16 or wider, within the bound.
No kernel may reach another device: no remote copies, remote signals or barrier semaphores. Data moves between devices by JAX's collectives and lax.ppermute only.
A program may use at most 128 MiB of HBM per device.

v0:
```python
import jax
import jax.numpy as jnp
from jax import lax
from jax.sharding import PartitionSpec as P

TILE = 128
PANEL = 1024


epsilon = 1e-06


def spread(value, axis, source):
    kept = jnp.where(lax.axis_index(axis) == source, value, 0).astype(value.dtype)
    return lax.psum(kept, axis)


def shards(token_ids, column_order, residual, attn_out, out_proj, norm_gain):
    section_count = lax.axis_size("section")
    tensor_count = lax.axis_size("tensor")
    section_id = lax.axis_index("section")
    tensor_id = lax.axis_index("tensor")
    model_width = out_proj.shape[0]
    span_rows = model_width // section_count
    span_cols = model_width // tensor_count
    projected = jnp.dot(
        lax.all_gather(attn_out, "tensor", axis=1, tiled=True),
        out_proj,
        preferred_element_type=jnp.float32,
    )
    rounded = (residual.astype(jnp.float32) + projected).astype(jnp.bfloat16)
    hidden = lax.optimization_barrier(rounded).astype(jnp.float32)
    squares = lax.psum(jnp.sum(hidden * hidden, axis=1), "tensor")
    kept_rows = (token_ids != 0).astype(jnp.float32)
    token_count = lax.psum(jnp.sum(kept_rows), "section")
    row_scale = lax.rsqrt(squares / model_width + epsilon) * kept_rows
    normed = (hidden * row_scale[:, None] * norm_gain[None, :]).astype(jnp.bfloat16)
    target = jnp.arange(section_count, dtype=jnp.int32)[:, None, None]
    tile_index = jnp.arange(span_rows // TILE, dtype=jnp.int32)[None, :, None]
    offset = jnp.arange(TILE, dtype=jnp.int32)[None, None, :]
    send_global = ((tile_index * section_count + target) * TILE + offset).reshape(model_width)
    col_tiles = jnp.arange(span_cols // TILE, dtype=jnp.int32)[:, None]
    cols_global = (
        (col_tiles * tensor_count + tensor_id) * TILE + jnp.arange(TILE, dtype=jnp.int32)[None, :]
    ).reshape(span_cols)
    full_rows = lax.all_gather(normed, "tensor", axis=1, tiled=True)
    outgoing = jnp.take(full_rows, jnp.take(column_order, send_global), axis=1)
    mine_rows = lax.all_to_all(outgoing, "section", split_axis=1, concat_axis=0, tiled=True)
    col_part = jnp.take(full_rows, jnp.take(column_order, cols_global), axis=1)
    gram_sum = lax.dot_general(
        mine_rows,
        lax.all_gather(col_part, "section", axis=0, tiled=True),
        (((0,), (0,)), ((), ())),
        preferred_element_type=jnp.float32,
    )
    hessian = gram_sum / token_count
    panel_local = PANEL // tensor_count
    per_group = panel_local // TILE
    gathered = lax.all_gather(hessian[:, :panel_local], "tensor", axis=1, tiled=True)
    panel_rows = (
        gathered.reshape(span_rows, tensor_count, per_group, TILE)
        .transpose(0, 2, 1, 3)
        .reshape(span_rows, PANEL)
    )
    first_tile = panel_rows[:TILE]
    stacked = lax.all_gather(first_tile, "section", axis=0, tiled=True)
    diag_block = stacked[:PANEL]
    chol_low = jnp.linalg.cholesky(diag_block)
    own_lower = lax.linalg.triangular_solve(
        chol_low, panel_rows, left_side=False, lower=True, transpose_a=True
    )
    copies = [
        spread(own_lower, "section", tensor_id + second * tensor_count)
        for second in range(section_count // tensor_count)
    ]
    shaped = [copy_rows.reshape(span_rows // TILE, TILE, PANEL) for copy_rows in copies]
    other_lower = jnp.stack(shaped, axis=1).reshape(span_cols, PANEL)
    row_tiles = jnp.arange(span_rows // TILE, dtype=jnp.int32)[:, None]
    rows_global = (
        (row_tiles * section_count + section_id) * TILE + jnp.arange(TILE, dtype=jnp.int32)[None, :]
    ).reshape(span_rows)
    panel_global = cols_global[:panel_local]
    left_part = jnp.take(own_lower, panel_global, axis=1)
    left_part = jnp.where(
        rows_global[:, None] >= panel_global[None, :], left_part, jnp.float32(0.0)
    )
    update = jnp.dot(
        own_lower,
        other_lower[panel_local:].T,
        precision=lax.Precision.HIGHEST,
        preferred_element_type=jnp.float32,
    )
    right_part = hessian[:, panel_local:] - update
    return jnp.concatenate([left_part, right_part], axis=1)


def solution(mesh):
    placed = (
        P("section"),
        P(),
        P("section", "tensor"),
        P("section", "tensor"),
        P(None, "tensor"),
        P("tensor"),
    )
    return jax.shard_map(
        shards, mesh=mesh, in_specs=placed, out_specs=P("section", "tensor"), check_vma=False
    )
```

profile of v0, /device:TPU:1, one launch (start us, length us, event | category | flops | bytes accessed | tf_op | source)
XLA Modules:
  0.0 999.4 jit_solution(9918803187925176559)
XLA Ops:
  7.3 76.7 %all-gather.6.cloned.1.call-done = bf16[256,8192]{1,0:T(8,128)(2,1)} async-done(((bf16[256,1024]{1,0:T(8,128)(2,1)}), bf16[256,8192]{1,0:T(8,128)(2,1)}) %all-gather.6.cloned.1.call-update) | async-done | bytes 4194320 | tf_op jit(solution)/shard_map/all_gather | solution.py:27
  84.0 11.5 %fusion.5 = bf16[256,1024]{1,0:T(8,128)(2,1)S(1)} fusion(bf16[256,8192]{1,0:T(8,128)(2,1)} %all-gather.6.cloned.1.call-done, bf16[8192,1024]{1,0:T(8,128)(2,1)} %param.10, bf16[256,1024]{1,0:T(8,128)(2,1)} %param.8), kind=kOutput, calls=%fused_computation.21 | convolution fusion | flops 4295753728 | bytes 22020096 | tf_op jit(solution)/shard_map/dot_general | solution.py:26
  95.7 16.3 %psum.28 = f32[256]{0:T(256)S(1)} all-reduce(f32[256]{0:T(256)S(1)} %fusion.6), channel_id=1, replica_groups=mesh['section'=16,'tensor'=8] {'tensor'}, use_global_device_ids=true, to_apply=%region_1.0 | all-reduce | flops 256 | bytes 2048 | tf_op jit(solution)/shard_map/psum | solution.py:33
  120.1 67.5 %all-gather.8.cloned.1.call-done = bf16[256,8192]{1,0:T(8,128)(2,1)} async-done(((bf16[256,1024]{1,0:T(8,128)(2,1)}), bf16[256,8192]{1,0:T(8,128)(2,1)}) %all-gather.8.cloned.1.call-update) | async-done | bytes 4194320 | tf_op jit(solution)/shard_map/all_gather | solution.py:46
  201.4 45.5 %gather_fusion = s32[8192]{0:T(1024)S(1)} fusion(s32[8192]{0:T(1024)S(1)} %copy-done, s32[8192]{0:T(1024)S(1)} %broadcast_clamp_fusion.1), kind=kCustom, calls=%fused_computation | custom fusion | bytes 98304 | tf_op jit(solution)/shard_map/jit(_take)/gather | solution.py:47
  247.1 33.8 %gather_fusion.1 = bf16[8192,256]{1,0:T(8,128)(2,1)} fusion(bf16[256,8192]{0,1:T(8,128)(2,1)} %copy.13, s32[8192]{0:T(1024)S(1)} %broadcast_clamp_fusion), kind=kCustom, calls=%fused_computation.1 | custom fusion | bytes 8421376 | tf_op jit(solution)/shard_map/jit(_take)/gather | solution.py:47
  297.5 70.7 %psum.29 = f32[]{:T(128)} all-reduce(f32[]{:T(128)} %get-tuple-element.74), channel_id=1, replica_groups=mesh['section'=16,'tensor'=8] {'section'}, use_global_device_ids=true, to_apply=%region_3.0 | all-reduce | flops 1 | bytes 8 | tf_op jit(solution)/shard_map/psum | solution.py:35
  379.1 51.6 %all-gather.12.cloned.1.call-done = f32[512,1024]{0,1:T(8,128)} async-done(((f32[512,128]{0,1:T(8,128)}), f32[512,1024]{0,1:T(8,128)}) %all-gather.12.cloned.1.call-update) | async-done | bytes 2097168 | tf_op jit(solution)/shard_map/all_gather | solution.py:59
  432.7 61.5 %all-gather.14.cloned.1.call-done = f32[2048,1024]{0,1:T(8,128)} async-done(((f32[128,1024]{0,1:T(8,128)}), f32[2048,1024]{0,1:T(8,128)}) %all-gather.14.cloned.1.call-update) | async-done | bytes 8388624 | tf_op jit(solution)/shard_map/all_gather | solution.py:66
  511.2 11.7 %cholesky.223 = f32[128,128]{1,0:T(8,128)S(1)} custom-call(f32[128,128]{1,0:T(8,128)S(1)} %cholesky.580), custom_call_target="Cholesky" | custom-call | tf_op jit(solution)/shard_map/jit(cholesky)/cholesky | solution.py:68
  522.9 9.8 custom-call.62
  539.2 11.9 %cholesky.244 = f32[128,128]{1,0:T(8,128)S(1)} custom-call(f32[128,128]{1,0:T(8,128)S(1)} %cholesky.584), custom_call_target="Cholesky" | custom-call | tf_op jit(solution)/shard_map/jit(cholesky)/cholesky | solution.py:68
  551.7 9.8 custom-call.63
  564.9 11.7 %cholesky.468 = f32[128,128]{1,0:T(8,128)S(1)} custom-call(f32[128,128]{1,0:T(8,128)S(1)} %cholesky.589), custom_call_target="Cholesky" | custom-call | tf_op jit(solution)/shard_map/jit(cholesky)/cholesky | solution.py:68
  577.9 9.8 custom-call.64
  591.2 11.9 %cholesky.487 = f32[128,128]{1,0:T(8,128)S(1)} custom-call(f32[128,128]{1,0:T(8,128)S(1)} %cholesky.594), custom_call_target="Cholesky" | custom-call | tf_op jit(solution)/shard_map/jit(cholesky)/cholesky | solution.py:68
  617.7 11.7 %cholesky.506 = f32[128,128]{1,0:T(8,128)S(1)} custom-call(f32[128,128]{1,0:T(8,128)S(1)} %cholesky.599), custom_call_target="Cholesky" | custom-call | tf_op jit(solution)/shard_map/jit(cholesky)/cholesky | solution.py:68
  630.7 10.2 %custom-call.66 = f32[1,128,128]{1,2,0:T(8,128)S(1)} custom-call(f32[1,128,128]{2,1,0:T(8,128)S(1)} %get-tuple-element.61), custom_call_target="InvertDiagBlocksLowerTriangular" | custom-call | tf_op jit(solution)/shard_map/jit(cholesky)/cholesky | solution.py:68
  644.2 11.7 %cholesky.526 = f32[128,128]{1,0:T(8,128)S(1)} custom-call(f32[128,128]{1,0:T(8,128)S(1)} %cholesky.604), custom_call_target="Cholesky" | custom-call | tf_op jit(solution)/shard_map/jit(cholesky)/cholesky | solution.py:68
  670.0 11.9 %cholesky.546 = f32[128,128]{1,0:T(8,128)S(1)} custom-call(f32[128,128]{1,0:T(8,128)S(1)} %cholesky.609), custom_call_target="Cholesky" | custom-call | tf_op jit(solution)/shard_map/jit(cholesky)/cholesky | solution.py:68
  695.7 11.7 %cholesky.564 = f32[128,128]{1,0:T(8,128)S(1)} custom-call(f32[128,128]{1,0:T(8,128)S(1)} %convolution_subtract_fusion.13), custom_call_target="Cholesky" | custom-call | tf_op jit(solution)/shard_map/jit(cholesky)/cholesky | solution.py:68
  719.2 22.9 %while.1 = (s32[]{:T(128)}, f32[1024,1024]{1,0:T(8,128)}, s32[8,2]{0,1:T(2,128)S(1)}, f32[8,128,128]{2,1,0:T(8,128)S(1)}, s32[]{:T(128)}) while((s32[]{:T(128)}, f32[1024,1024]{1,0:T(8,128)}, s32[8,2]{0,1:T(2,128)S(1)}, f32[8,128,128]{2,1,0:T(8,128)S(1)}, s32[]{:T(128)}) %tuple.59), condition=%wide.while_cond, body=%wide.while_body.sunk | while | flops 2 | bytes 131181 | solution.py:69
  742.1 78.8 %custom-call.69 = f32[8,128,128]{1,2,0:T(8,128)S(1)} custom-call(f32[8,128,128]{2,1,0:T(8,128)S(1)} %get-tuple-element.12), custom_call_target="InvertDiagBlocksLowerTriangular" | custom-call | tf_op jit(solution)/shard_map/triangular_solve | solution.py:69
  847.8 133.4 %all-reduce.4.cloned.1.call-done = (f32[4,1,128,1024]{3,2,1,0:T(8,128)}, f32[4,1,128,1024]{3,2,1,0:T(8,128)}) async-done(((f32[4,1,128,1024]{3,2,1,0:T(8,128)}, f32[4,1,128,1024]{3,2,1,0:T(8,128)}), (f32[4,1,128,1024]{3,2,1,0:T(8,128)}, f32[4,1,128,1024]{3,2,1,0:T(8,128)})) %all-reduce.4.cloned.1.call-update) | async-done | bytes 4194320 | tf_op jit(solution)/shard_map/psum | solution.py:15
  (160 shorter events, 198.8 us)
Async XLA Ops:
  6.5 107.3 %copy-start = (s32[8192]{0:T(1024)S(1)}, s32[8192]{0:T(1024)}, u32[]{:S(2)}) copy-start(s32[8192]{0:T(1024)} %param.7) | copy-start | bytes 98308
  6.5 77.5 %all-gather.6.cloned.1.call-start = ((), (), s32[]{:S(2)}) async-start(), calls=%async_computation.1 | async-start | bytes 4718592 | tf_op jit(solution)/shard_map/all_gather | solution.py:27
  7.3 104.7 %copy-start.7 = (s32[256]{0:T(256)S(1)}, s32[256]{0:T(256)}, u32[]{:S(2)}) copy-start(s32[256]{0:T(256)} %param.6) | copy-start | bytes 3076
  7.3 105.4 %copy-start.6 = (f32[1024]{0:T(1024)S(1)}, f32[1024]{0:T(1024)}, u32[]{:S(2)}) copy-start(f32[1024]{0:T(1024)} %param.11) | copy-start | bytes 12292
  7.3 180.3 %all-gather.8.cloned.1.call-start = ((), (), s32[]{:S(2)}) async-start(), calls=%async_computation.2 | async-start | bytes 4718592 | tf_op jit(solution)/shard_map/all_gather | solution.py:46
  113.7 254.4 %all-gather.10.cloned.1.call-start = ((), (), s32[]{:S(2)}) async-start(), calls=%async_computation.3 | async-start | bytes 8912896 | tf_op jit(solution)/shard_map/all_gather | solution.py:52
  291.8 76.3 %all-to-all-start = ((bf16[256,16,512]{2,0,1:T(8,128)(2,1)}), bf16[256,16,512]{2,0,1:T(8,128)(2,1)}, u32[]{:S(2)}, u32[]{:S(2)}) async-start(bf16[256,16,512]{2,0,1:T(8,128)(2,1)} %broadcast_select_fusion), calls=%async_computation | async-start | bytes 8388608 | tf_op jit(solution)/shard_map/all_to_all | solution.py:48
  297.4 133.3 %all-gather.12.cloned.1.call-start = ((), (), s32[]{:S(2)}) async-start(), calls=%async_computation.4 | async-start | bytes 2359296 | tf_op jit(solution)/shard_map/all_gather | solution.py:59
  377.0 1.3 copy-start.3
  379.1 115.1 %all-gather.14.cloned.1.call-start = ((), (), s32[]{:S(2)}) async-start(), calls=%async_computation.5 | async-start | bytes 8912896 | tf_op jit(solution)/shard_map/all_gather | solution.py:66
  432.6 548.6 %all-reduce.4.cloned.1.call-start = ((), (), s32[]{:S(2)}) async-start(), calls=%async_computation.6 | async-start | bytes 8388608 | tf_op jit(solution)/shard_map/psum | solution.py:15
  509.1 2.0 copy-start.2
  822.3 6.1 copy-start.5
  981.2 2.9 copy-start.4
  984.1 8.0 copy-start.1
Sparse Core Ops, SparseCore 0:
  9.7 74.2 all-gather.5
  113.8 73.7 all-gather.7
  201.3 59.5 all-gather.9
  379.2 51.4 all-gather.11
  432.7 61.3 all-gather.13
  847.0 134.2 all-reduce.3
where the time goes:
time: 1010 us; the launch traced here: 999 us
  waiting for transfers between devices  391 us (39%)
  other arithmetic  274 us (27%)
  local copies, waits for them, and re-layouts  155 us (15%)
  blocking collectives  87 us (9%)
  matrix products  66.4 us (7%)
  between operations  19.4 us (2%)
    another operation x30, other arithmetic, shards(): chol_low = jnp.linalg.cholesky(diag_block)  172 us
    psum x1, waiting for transfers between devices, spread(): return lax.psum(kept, axis)  133 us
    gather x4, local copies, waits for them, and re-layouts, shards(): outgoing = jnp.take(full_rows, jnp.take(column_order, send_global), axis=1)  85.8 us
    another operation x3, other arithmetic, shards(): lax.linalg.triangular_solve(chol_low, panel_rows, left_side=False, lower=...  83.7 us
    all_gather x1, waiting for transfers between devices, shards(): lax.all_gather(attn_out, 'tensor', axis=1, tiled=True)  76.7 us
    psum x1, blocking collectives, shards(): token_count = lax.psum(jnp.sum(kept_rows), 'section')  70.7 us
    all_gather x1, waiting for transfers between devices, shards(): full_rows = lax.all_gather(normed, 'tensor', axis=1, tiled=True)  67.5 us
    all_gather x1, waiting for transfers between devices, shards(): stacked = lax.all_gather(first_tile, 'section', axis=0, tiled=True)  61.5 us
  transfers between devices with their start and end apart: 7, of which 5 were waited for; matrix products, arithmetic and copies ran while one was open for 10% of the time, Pallas kernels for 0%

commit v1 on v0

v1 whole, which is shorter than its diff:
```python
import functools

import jax
import jax.numpy as jnp
from jax import lax
from jax.experimental import pallas as pl
from jax.experimental.pallas import tpu as pltpu
from jax.sharding import PartitionSpec as P

TILE = 128
PANEL = 1024
WIDTH = 8192
TOK = 256
EXT = 16
epsilon = 1e-06
F32 = jnp.float32
BF16 = jnp.bfloat16
KEYS = [(0, 0), (0, 1), (1, 0), (1, 1), (3, 0), (3, 1), (2, 0), (2, 1)]
CHUNK = {(d, f): d * 2 + f for d in range(4) for f in range(2)}
MIB = 1024 * 1024


def params(limit=48):
    return pltpu.CompilerParams(vmem_limit_bytes=limit * MIB)


def shift_t(value, dx, dy):
    pairs = [(t, ((t // 4) ^ dy) * 4 + (t % 4 + dx) % 4) for t in range(8)]
    return lax.ppermute(value, "tensor", pairs)


def shift_s(value, dz, dy, dc=0):
    pairs = [(s, ((s // 4 + dz) % 4) * 4 + ((s % 4) ^ (2 * dy + dc))) for s in range(16)]
    return lax.ppermute(value, "section", pairs)


def gather8(x, shift, half):
    b = shift(x, 0, 1)
    ra, la = shift(x, 1, 0), shift(x, 3, 0)
    rb, lb = shift(b, 1, 0), shift(b, 3, 0)
    fa = [shift(ra[:half], 1, 0), shift(la[half:], 3, 0)]
    fb = [shift(rb[:half], 1, 0), shift(lb[half:], 3, 0)]
    return [[x], [b], [ra], [rb], [la], [lb], fa, fb]


def flatten(shards):
    arrays, meta = [], []
    for pieces in shards:
        off, entry = 0, []
        for piece in pieces:
            entry.append((len(arrays), off, piece.shape[0]))
            arrays.append(piece)
            off += piece.shape[0]
        meta.append(entry)
    return arrays, meta


def nt(a, b):
    return lax.dot_general(a, b, (((1,), (1,)), ((), ())), preferred_element_type=F32)


def nn(a, b):
    return lax.dot_general(a, b, (((1,), (0,)), ((), ())), preferred_element_type=F32)


def split(a):
    hi = a.astype(BF16)
    return hi, (a - hi.astype(F32)).astype(BF16)


def dot3(op, a, b):
    return op(a[0], b[0]) + (op(a[0], b[1]) + op(a[1], b[0]))


def project(shards, out_proj, origins, acc=None, residual=None):
    arrays, meta = flatten(shards)
    n = len(shards)
    final = residual is not None
    cols = out_proj.shape[1]

    def body(*refs):
        _, w_ref, *rest = refs
        pieces, rest = rest[: len(arrays)], rest[len(arrays) :]
        if acc is not None:
            acc_ref, *rest = rest
        if final:
            res_ref, *rest = rest
        out_ref, acc_s = rest
        i = pl.program_id(0)

        @pl.when(i == 0)
        def _():
            acc_s[...] = acc_ref[...] if acc is not None else jnp.zeros_like(acc_s)

        for r in range(n):

            @pl.when(i == r)
            def _(r=r):
                for j, off, size in meta[r]:
                    size = min(size, TOK - off)
                    acc_s[off : off + size, :] += nn(pieces[j][:size, :], w_ref[...])

        @pl.when(i == n - 1)
        def _():
            if final:
                h = (res_ref[...].astype(F32) + acc_s[...]).astype(BF16).astype(F32)
                out_ref[...] = h.T.astype(BF16)
            else:
                out_ref[...] = acc_s[...]

    whole = lambda shape: pl.BlockSpec(shape, lambda i, o: (0,) * len(shape))
    operands = [out_proj, *arrays]
    specs = [pl.BlockSpec((1024, cols), lambda i, o: (o[i], 0))] + [whole(a.shape) for a in arrays]
    if acc is not None:
        operands.append(acc)
        specs.append(whole(acc.shape))
    if final:
        operands.append(residual)
        specs.append(whole(residual.shape))
    shape = (cols, TOK) if final else (TOK, cols)
    return pl.pallas_call(
        body,
        out_shape=jax.ShapeDtypeStruct(shape, BF16 if final else F32),
        grid_spec=pltpu.PrefetchScalarGridSpec(
            num_scalar_prefetch=1,
            grid=(n,),
            in_specs=specs,
            out_specs=whole(shape),
            scratch_shapes=[pltpu.VMEM((TOK, cols), F32)],
        ),
        compiler_params=params(),
        cost_estimate=pl.CostEstimate(flops=2 * TOK * 1024 * cols * n, bytes_accessed=n * 2 * MIB, transcendentals=0),
        name="project",
    )(origins, *operands)


def select(shards, gains, origins, index, kept):
    arrays, meta = flatten(shards)
    n_cols, n_rows = 1024, 512

    def body(*refs):
        origin, index_ref, kept_ref, *rest = refs
        pieces, rest = rest[: len(arrays)], rest[len(arrays) :]
        gain_refs, rest = rest[:8], rest[8:]
        cols_ref, rows0_ref, rows1_ref, pan_ref, nrm = rest
        step = 128

        def squares(ref, size, total):
            def add(c, total):
                v = ref[pl.ds(pl.multiple_of(c * step, step), step), :].astype(F32)
                return total + jnp.sum((v * v).reshape(step // 8, 8, TOK), axis=0)

            return lax.fori_loop(0, size // step, add, total)

        total = jnp.zeros((8, TOK), F32)
        for r in range(8):
            for j, off, size in meta[r]:
                total = squares(pieces[j], size, total)
        scale = lax.rsqrt(jnp.sum(total, axis=0, keepdims=True) / WIDTH + epsilon) * kept_ref[...]
        for r in range(8):
            g = jnp.sum(gain_refs[r][...].astype(F32), axis=0, keepdims=True)
            gain = jnp.broadcast_to(g, (8, 1024)).T[:, :1]
            for j, off, size in meta[r]:
                for c in range(size // step):
                    h = pieces[j][c * step : (c + 1) * step, :].astype(F32)
                    at = off + c * step
                    nrm[r * 1024 + at : r * 1024 + at + step, :] = (h * scale * gain[at : at + step, :]).astype(BF16)

        def pick(start, size):
            idx = index_ref[pl.ds(start, size), :]
            lane = lax.broadcasted_iota(jnp.int32, (size, 1024), 1)
            acc = jnp.zeros((size, TOK), F32)
            for r in range(8):
                hot = jnp.where(idx - origin[r] * 1024 == lane, 1.0, 0.0).astype(BF16)
                acc += nn(hot, nrm[r * 1024 : (r + 1) * 1024, :])
            return acc.astype(BF16)

        pan_ref[:TILE, :] = pick(0, TILE)
        first = lax.broadcasted_iota(jnp.int32, (EXT, TOK), 0) == 0
        pan_ref[TILE:, :] = jnp.where(first, kept_ref[...], 0.0).astype(BF16)

        def fill(ref, base):
            def one(c, _):
                at = pl.multiple_of(c * 256, 256)
                ref[pl.ds(at, 256), :] = pick(pl.multiple_of(base + c * 256, 128), 256)
                return 0

            lax.fori_loop(0, ref.shape[0] // 256, one, 0)

        fill(rows1_ref, TILE)
        fill(rows0_ref, TILE + n_rows)
        fill(cols_ref, TILE + 2 * n_rows)

    vm = pl.BlockSpec(memory_space=pltpu.VMEM)
    gain_arrays = [g for g, _ in gains]
    gain_specs = [pl.BlockSpec((EXT, 1024), functools.partial(lambda b, i: (b, 0), b)) for _, b in gains]
    outs = [(n_cols, TOK), (n_rows, TOK), (n_rows, TOK), (TILE + EXT, TOK)]
    return pl.pallas_call(
        body,
        grid=(1,),
        out_shape=[jax.ShapeDtypeStruct(s, BF16) for s in outs],
        in_specs=[pl.BlockSpec(memory_space=pltpu.SMEM), vm, vm] + [vm] * len(arrays) + gain_specs,
        out_specs=[vm] * 4,
        scratch_shapes=[pltpu.VMEM((WIDTH, TOK), BF16)],
        compiler_params=params(),
        cost_estimate=pl.CostEstimate(flops=2 * 2176 * WIDTH * TOK, bytes_accessed=8 * MIB, transcendentals=0),
        name="select",
    )(origins, index, kept, *arrays, *gain_arrays)


def place(pieces, meta, slot, scratch):
    for r in range(8):
        row = pl.multiple_of(slot[r] * TILE, TILE)
        for j, off, size in meta[r]:
            for c in range(size):
                scratch[pl.ds(row, TILE), (off + c) * TOK : (off + c + 1) * TOK] = pieces[j][c]


def panel_gram(shards, slots):
    arrays, meta = flatten(shards)

    def body(slot, *refs):
        pieces, (pan_ref, gram_ref) = refs[: len(arrays)], refs[len(arrays) :]
        place(pieces, meta, slot, pan_ref)

        def one(c, _):
            rows = pl.ds(pl.multiple_of(c * 256, 256), 256)
            gram_ref[rows, :] = nt(pan_ref[rows, :], pan_ref[...])
            return 0

        lax.fori_loop(0, 4, one, 0)

    vm = pl.BlockSpec(memory_space=pltpu.VMEM)
    return pl.pallas_call(
        body,
        out_shape=[jax.ShapeDtypeStruct((PANEL, 2048), BF16), jax.ShapeDtypeStruct((PANEL, PANEL), F32)],
        in_specs=[pl.BlockSpec(memory_space=pltpu.SMEM)] + [vm] * len(arrays),
        out_specs=[vm] * 2,
        compiler_params=params(),
        cost_estimate=pl.CostEstimate(flops=2 * 1024 * 1024 * 2048, bytes_accessed=12 * MIB, transcendentals=0),
        name="panel_gram",
    )(slots, *arrays)


def block_gram(row_shards, col_shards, pan, slots):
    row_arrays, row_meta = flatten(row_shards)
    col_arrays, col_meta = flatten(col_shards)

    def body(slot, pan_ref, *refs):
        rp, refs = refs[: len(row_arrays)], refs[len(row_arrays) :]
        cp, refs = refs[: len(col_arrays)], refs[len(col_arrays) :]
        hk_ref, hs_ref, pk_ref, ps_ref, pc_ref, rows, cols = refs
        place(rp, row_meta, slot, rows)
        for key, entry in zip(KEYS, col_meta):
            lane = CHUNK[key] * TOK
            for j, off, size in entry:
                cols[off : off + size, lane : lane + TOK] = cp[j][...]

        def one(c, _):
            at = pl.ds(pl.multiple_of(c * 256, 256), 256)
            keep = rows[at, :]
            send = rows[pl.ds(pl.multiple_of(512 + c * 256, 256), 256), :]
            pk_ref[at, :] = nt(keep, pan_ref[...])
            ps_ref[at, :] = nt(send, pan_ref[...])
            hk_ref[at, :] = nt(keep, cols[...])
            hs_ref[at, :] = nt(send, cols[...])
            return 0

        lax.fori_loop(0, 2, one, 0)

        def two(c, _):
            at = pl.ds(pl.multiple_of(c * 256, 256), 256)
            pc_ref[at, :] = nt(cols[at, :], pan_ref[...])
            return 0

        lax.fori_loop(0, 4, two, 0)

    vm = pl.BlockSpec(memory_space=pltpu.VMEM)
    outs = [(512, 1024)] * 4 + [(1024, PANEL)]
    return pl.pallas_call(
        body,
        out_shape=[jax.ShapeDtypeStruct(s, F32) for s in outs],
        in_specs=[pl.BlockSpec(memory_space=pltpu.SMEM), vm] + [vm] * (len(row_arrays) + len(col_arrays)),
        out_specs=[vm] * 5,
        scratch_shapes=[pltpu.VMEM((1024, 2048), BF16)] * 2,
        compiler_params=params(),
        cost_estimate=pl.CostEstimate(flops=6 * 1024 * 1024 * 2048, bytes_accessed=24 * MIB, transcendentals=0),
        name="block_gram",
    )(slots, pan, *row_arrays, *col_arrays)


def factor_tile(a, groups=TILE // 8):
    lane = lax.broadcasted_iota(jnp.int32, (8, TILE), 1)
    sub = lax.broadcasted_iota(jnp.int32, (8, TILE), 0)
    A = [a[8 * g : 8 * g + 8, :] for g in range(groups)]
    E = [jnp.where(lane == sub + 8 * g, 1.0, 0.0).astype(F32) for g in range(groups)]
    for j in range(TILE):
        g0, s0 = divmod(j, 8)
        inv = 1.0 / A[g0][s0 : s0 + 1, j : j + 1]
        row = A[g0][s0 : s0 + 1, :] * inv
        erow = E[g0][s0 : s0 + 1, :] * inv
        for g in range(g0, groups):
            col = A[g][:, j : j + 1]
            if g == g0:
                if s0 == 7:
                    continue
                col = jnp.where(sub[:, :1] > s0, col, 0.0)
            A[g] = A[g] - col * row
            E[g] = E[g] - col * erow
    U, V = [], []
    for g in range(groups):
        diag = jnp.sum(jnp.where(lane == sub + 8 * g, A[g], 0.0), axis=1, keepdims=True)
        rs = lax.rsqrt(diag)
        U.append(jnp.where(lane >= sub + 8 * g, A[g] * rs, 0.0))
        V.append(E[g] * rs)
    return jnp.concatenate(U, axis=0), jnp.concatenate(V, axis=0)


def cholesky(gram, other, count):
    tiles = PANEL // TILE

    def body(count_ref, g_ref, o_ref, u_ref, v_ref, ph, plo, lh, ll):
        inv = 1.0 / count_ref[0]

        def load(c, _):
            rows = pl.ds(pl.multiple_of(c * 64, 64), 64)
            u_ref[rows, :] = (g_ref[rows, :] + o_ref[rows, :]) * inv
            return 0

        lax.fori_loop(0, PANEL // 64, load, 0)

        def step(k, _):
            at = pl.ds(pl.multiple_of(k * TILE, TILE), TILE)
            U, V = factor_tile(u_ref[at, at])
            v_ref[at, :] = V
            vs = split(V)
            panel = dot3(nn, vs, split(u_ref[at, :]))
            ph[...], plo[...] = split(panel)
            left = dot3(nt, split(u_ref[:, at]), vs)
            lh[...], ll[...] = split(left)
            u_ref[at, :] = panel
            u_ref[at, at] = U

            def update(j, _):
                rows = pl.ds(pl.multiple_of(j * TILE, TILE), TILE)
                u_ref[rows, :] -= dot3(nn, (lh[rows, :], ll[rows, :]), (ph[...], plo[...]))
                return 0

            lax.fori_loop(k + 1, tiles, update, 0)
            return 0

        lax.fori_loop(0, tiles, step, 0)

    vm = pl.BlockSpec(memory_space=pltpu.VMEM)
    return pl.pallas_call(
        body,
        out_shape=[jax.ShapeDtypeStruct((PANEL, PANEL), F32), jax.ShapeDtypeStruct((PANEL, TILE), F32)],
        in_specs=[pl.BlockSpec(memory_space=pltpu.SMEM), vm, vm],
        out_specs=[vm, vm],
        scratch_shapes=[pltpu.VMEM((TILE, PANEL), BF16)] * 2 + [pltpu.VMEM((PANEL, TILE), BF16)] * 2,
        compiler_params=params(),
        cost_estimate=pl.CostEstimate(flops=80_000_000_000, bytes_accessed=12 * MIB, transcendentals=0),
        name="cholesky",
    )(count, gram, other)


def finish(scalars, count, hk, hr, pk, pr, pc, pcr, u, v):
    tiles = PANEL // TILE

    def body(sc, count_ref, hk_ref, hr_ref, pk_ref, pr_ref, pc_ref, pcr_ref, u_ref, v_ref, out_ref, uh, ul, vh, vl, xh, xl, xr):
        inv = 1.0 / count_ref[0]

        def cut(c, _):
            rows = pl.ds(pl.multiple_of(c * 64, 64), 64)
            uh[rows, :], ul[rows, :] = split(u_ref[rows, :])
            vh[rows, :], vl[rows, :] = split(v_ref[rows, :])
            return 0

        lax.fori_loop(0, PANEL // 64, cut, 0)

        def solve(b):
            parts = []
            for k in range(tiles):
                rows = slice(k * TILE, (k + 1) * TILE)
                x = dot3(nt, split(b[:, :TILE]), (vh[rows, :], vl[rows, :]))
                parts.append(x)
                if k + 1 < tiles:
                    b = b[:, TILE:] - dot3(nn, split(x), (uh[rows, (k + 1) * TILE :], ul[rows, (k + 1) * TILE :]))
            return jnp.concatenate(parts, axis=1)

        def from_rows(c, _):
            rows = pl.ds(pl.multiple_of(c * 256, 256), 256)
            x = solve((pk_ref[rows, :] + pr_ref[rows, :]) * inv)
            xr[rows, :] = x
            xh[rows, :], xl[rows, :] = split(x)
            return 0

        lax.fori_loop(0, 2, from_rows, 0)

        def from_cols(c, _):
            rows = pl.ds(pl.multiple_of(c * 256, 256), 256)
            x = solve((pc_ref[rows, :] + pcr_ref[rows, :]) * inv)
            to = pl.ds(pl.multiple_of(512 + c * 256, 256), 256)
            xh[to, :], xl[to, :] = split(x)
            return 0

        lax.fori_loop(0, 4, from_cols, 0)

        def trail(c, _):
            rows = pl.ds(pl.multiple_of(c * 128, 128), 128)
            cols = slice(512 + TILE, 512 + 1024)
            up = dot3(nt, (xh[rows, :], xl[rows, :]), (xh[cols, :], xl[cols, :]))
            out_ref[rows, TILE:] = (hk_ref[rows, TILE:] + hr_ref[rows, TILE:]) * inv - up
            left = xr[rows, pl.ds(pl.multiple_of(sc[1] * TILE, TILE), TILE)]
            row = (c * 16 + sc[0]) * TILE + lax.broadcasted_iota(jnp.int32, (TILE, TILE), 0)
            col = sc[1] * TILE + lax.broadcasted_iota(jnp.int32, (TILE, TILE), 1)
            out_ref[rows, :TILE] = jnp.where(row >= col, left, 0.0)
            return 0

        lax.fori_loop(0, 4, trail, 0)

    vm = pl.BlockSpec(memory_space=pltpu.VMEM)
    sm = pl.BlockSpec(memory_space=pltpu.SMEM)
    return pl.pallas_call(
        body,
        out_shape=jax.ShapeDtypeStruct((512, 1024), F32),
        in_specs=[sm, sm] + [vm] * 8,
        out_specs=vm,
        scratch_shapes=[pltpu.VMEM((PANEL, PANEL), BF16)] * 2
        + [pltpu.VMEM((PANEL, TILE), BF16)] * 2
        + [pltpu.VMEM((1536, PANEL), BF16)] * 2
        + [pltpu.VMEM((512, PANEL), F32)],
        compiler_params=params(56),
        cost_estimate=pl.CostEstimate(flops=16_000_000_000, bytes_accessed=28 * MIB, transcendentals=0),
        name="finish",
    )(scalars, count, hk, hr, pk, pr, pc, pcr, u, v)


def shards_of(token_ids, column_order, residual, attn_out, out_proj, norm_gain):
    s = lax.axis_index("section").astype(jnp.int32)
    t = lax.axis_index("tensor").astype(jnp.int32)
    y, x = t // 4, t % 4
    z, yl, core = s // 4, (s // 2) % 2, s % 2

    def origin(dx, dy):
        return (y ^ dy) * 4 + (x - dx) % 4

    origins = jnp.stack([origin(*k) for k in KEYS])
    slots = jnp.stack([((o // 4) ^ core) * 4 + o % 4 for o in [origin(*k) for k in KEYS]])

    g_hi = lax.reduce_precision(norm_gain, 8, 7)
    g_mid = lax.reduce_precision(norm_gain - g_hi, 8, 7)
    g_lo = norm_gain - g_hi - g_mid
    parts = jnp.stack([g_hi, g_mid, g_lo]).astype(BF16)
    ext = jnp.concatenate([parts, jnp.zeros((EXT - 3, 1024), BF16)], axis=0)
    own = jnp.concatenate([attn_out, ext], axis=0)
    a = gather8(own, shift_t, 144)

    acc = project(a[:2], out_proj, origins[:2])
    acc = project(a[2:6], out_proj, origins[2:6], acc)
    hidden = project(a[6:], out_proj, origins[6:], acc, residual)

    gains = []
    for pieces in a:
        last = pieces[-1]
        gains.append((last, last.shape[0] // EXT - 1))

    tiles = [t]
    for dy in (1, 0):
        for dz in range(4):
            group = ((z + dz) % 4) * 2 + (yl ^ dy)
            tiles.append(16 * x + 2 * group + y)
    tiles += [j * 8 + t for j in range(8)]
    index = jnp.take(column_order.reshape(64, TILE), jnp.stack(tiles), axis=0).reshape(-1, 1)
    kept = (token_ids != 0).astype(F32).reshape(1, TOK)

    h = gather8(hidden, shift_t, 512)
    cols, rows0, rows1, pan = select(h, gains, origins, index, kept)

    pan2 = jnp.stack([pan, shift_s(pan, 0, 1)])
    pan8 = jnp.concatenate([pan2] + [shift_s(pan2, dz, 0) for dz in (1, 2, 3)], axis=0)
    kept_here = jnp.sum(pan8[:, TILE : TILE + 1, :].astype(F32))
    count = (kept_here + shift_s(kept_here.reshape(1, 1), 0, 0, 1)[0, 0]).reshape(1)
    pan_shards = gather8(pan8[:, :TILE, :], shift_t, 4)

    theirs = shift_s(rows1, 0, 1).reshape(4, TILE, TOK)
    mine = rows0.reshape(4, TILE, TOK)
    both = jnp.stack([mine, theirs], axis=1)
    rows8 = jnp.concatenate([both[0]] + [shift_s(both[dz], dz, 0) for dz in (1, 2, 3)], axis=0)
    row_shards = gather8(rows8, shift_t, 4)
    col_shards = gather8(cols, shift_s, 512)

    pan_all, gram = panel_gram(pan_shards, origins)
    gram_other = shift_s(gram, 0, 0, 1)
    hk, hs, pk, ps, pc = block_gram(row_shards, col_shards, pan_all, slots)
    u, v = cholesky(gram, gram_other, count)
    hr, pr, pcr = [shift_s(w, 0, 0, 1) for w in (hs, ps, pc)]
    return finish(jnp.stack([s, t]), count, hk, hr, pk, pr, pc, pcr, u, v)


def solution(mesh):
    placed = (
        P("section"),
        P(),
        P("section", "tensor"),
        P("section", "tensor"),
        P(None, "tensor"),
        P("tensor"),
    )
    return jax.shard_map(
        shards_of, mesh=mesh, in_specs=placed, out_specs=P("section", "tensor"), check_vma=False
    )
```

time: 1010 us -> 437 us (0.43)
  other arithmetic: 274 us -> 2.45 us
  waiting for transfers between devices: 391 us -> 123 us
  Pallas kernels: 0 us -> 205 us
  local copies, waits for them, and re-layouts: 155 us -> 22.9 us
  blocking collectives: 87 us -> 0 us
  starting transfers between devices: 5.79 us -> 72.9 us
  matrix products: 66.4 us -> 0 us
  between operations: 19.4 us -> 2.72 us
    all_gather x5 -> x0, waiting for transfers between devices: 257 us -> none  [the longest x1 76.7 us: shards(): lax.all_gather(attn_out, 'tensor', axis=1, tiled=True)]
    another operation x34 -> x6, other arithmetic: 259 us -> 1.56 us  [the longest x30 172 us: shards(): chol_low = jnp.linalg.cholesky(diag_block)]
    pallas_call x0 -> x8, Pallas kernels: none -> 205 us  [the longest x1 104 us: cholesky(): pl.pallas_call(body, out_shape=[jax.ShapeDtypeStruct((PANEL, PANEL), F32)...]
    psum x1 -> x0, waiting for transfers between devices: 133 us -> none  [spread(): return lax.psum(kept, axis)]
    ppermute x0 -> x58, waiting for transfers between devices: none -> 123 us  [the longest x36 86.1 us: shift_t(): return lax.ppermute(value, 'tensor', pairs)]
    gather x7 -> x1, local copies, waits for them, and re-layouts: 98.9 us -> 0.56 us  [shards_of(): jnp.take(column_order.reshape(64, TILE), jnp.stack(tiles), axis=0)]
    psum x2 -> x0, blocking collectives: 87 us -> none  [the longest x1 70.7 us: shards(): token_count = lax.psum(jnp.sum(kept_rows), 'section')]
    ppermute x0 -> x58, starting transfers between devices: none -> 72.9 us  [the longest x36 40 us: shift_t(): return lax.ppermute(value, 'tensor', pairs)]
  transfers between devices with their start and end apart: 7 -> 58, of which waited for: 5 -> 28; matrix products, arithmetic and copies ran while one was open for 10% -> 2% of each run, Pallas kernels for 0% -> 32%
where the time goes in v1:
time: 437 us; the launch traced here: 428 us
  Pallas kernels  205 us (47%)
  waiting for transfers between devices  123 us (28%)
  starting transfers between devices  72.9 us (17%)
  local copies, waits for them, and re-layouts  22.9 us (5%)
    pallas_call x1, Pallas kernels, cholesky(): pl.pallas_call(body, out_shape=[jax.ShapeDtypeStruct((PANEL, PANEL), F32)...  104 us
    ppermute x36, waiting for transfers between devices, shift_t(): return lax.ppermute(value, 'tensor', pairs)  86.1 us
    pallas_call x1, Pallas kernels, finish(): pl.pallas_call(body, out_shape=jax.ShapeDtypeStruct((512, 1024), F32), in...  40.9 us
    ppermute x36, starting transfers between devices, shift_t(): return lax.ppermute(value, 'tensor', pairs)  40 us
    ppermute x22, waiting for transfers between devices, shift_s(): return lax.ppermute(value, 'section', pairs)  36.7 us
    ppermute x22, starting transfers between devices, shift_s(): return lax.ppermute(value, 'section', pairs)  32.9 us
    pallas_call x1, Pallas kernels, block_gram(): pl.pallas_call(body, out_shape=[jax.ShapeDtypeStruct(s, F32) for s in out...  21.7 us
    pallas_call x1, Pallas kernels, select(): pl.pallas_call(body, grid=(1,), out_shape=[jax.ShapeDtypeStruct(s, BF16)...  16 us
  transfers between devices with their start and end apart: 58, of which 28 were waited for; matrix products, arithmetic and copies ran while one was open for 2% of the time, Pallas kernels for 32%

profile of v1, /device:TPU:1, one launch (start us, length us, event | category | flops | bytes accessed | tf_op | source)
XLA Modules:
  0.0 428.5 jit_solution(9565051878721806119)
XLA Ops:
  2.9 3.8 collective-permute-start.4
  9.2 9.6 %collective-permute-done.4.refs_3_.refs_14_ = bf16[272,1024]{1,0:T(8,128)(2,1)S(1)} collective-permute-done((bf16[272,1024]{1,0:T(8,128)(2,1)S(1)}, bf16[272,1024]{1,0:T(8,128)(2,1)S(1)}, u32[]{:S(2)}, u32[]{:S(2)}) %collective-permute-start.4) | collective-permute-done | bytes 557088 | tf_op jit(solution)/shard_map/ppermute | solution.py:29
  24.4 7.3 %collective-permute-done.7.refs_5_.refs_18_ = bf16[272,1024]{1,0:T(8,128)(2,1)S(1)} collective-permute-done((bf16[272,1024]{1,0:T(8,128)(2,1)S(1)}, bf16[272,1024]{1,0:T(8,128)(2,1)S(1)}, u32[]{:S(2)}, u32[]{:S(2)}) %collective-permute-start.7) | collective-permute-done | bytes 557088 | tf_op jit(solution)/shard_map/ppermute | solution.py:29
  38.9 6.1 %project.4.refs_6_ = f32[256,1024]{1,0:T(8,128)S(1)} custom-call(s32[4]{0:T(128)S(1)} %pad_add_fusion.2.refs_0_, bf16[8192,1024]{1,0:T(8,128)(2,1)} %refs_1_.5, bf16[272,1024]{1,0:T(8,128)(2,1)S(1)} %collective-permute-done.refs_2_.refs_15_, bf16[272,1024]{1,0:T(8,128)(2,1)S(1)} %collective-permute-done.5.refs_3_.refs_16_, ...), custom_call_target="tpu_custom_call" | custom-call | flops 2147483648 | bytes 8388608 | tf_op jit(solution)/shard_map/project/pallas_call | solution.py:121
  47.4 3.9 project.5.refs_3_
  56.0 7.7 %collective-permute-done.9.refs_4_ = bf16[1024,256]{1,0:T(8,128)(2,1)} collective-permute-done((bf16[1024,256]{1,0:T(8,128)(2,1)S(1)}, bf16[1024,256]{1,0:T(8,128)(2,1)}, u32[]{:S(2)}, u32[]{:S(2)}) %collective-permute-start.9) | collective-permute-done | bytes 524320 | tf_op jit(solution)/shard_map/ppermute | solution.py:29
  68.8 8.5 %collective-permute-done.13.refs_8_ = bf16[1024,256]{1,0:T(8,128)(2,1)S(1)} collective-permute-done((bf16[1024,256]{1,0:T(8,128)(2,1)}, bf16[1024,256]{1,0:T(8,128)(2,1)S(1)}, u32[]{:S(2)}, u32[]{:S(2)}) %collective-permute-start.13) | collective-permute-done | bytes 524320 | tf_op jit(solution)/shard_map/ppermute | solution.py:29
  84.9 3.8 collective-permute-done.17.refs_12_
  90.0 16.0 %select.83 = (bf16[1024,256]{1,0:T(8,128)(2,1)S(1)}, bf16[512,256]{1,0:T(8,128)(2,1)S(1)}, bf16[512,256]{1,0:T(8,128)(2,1)S(1)}, bf16[144,256]{1,0:T(8,128)(2,1)S(1)}) custom-call(s32[8]{0:T(128)S(1)} %stack.190.refs_0_.slot, s32[2176,1]{1,0:T(8,128)} %bitcast.81, f32[1,256]{1,0:T(1,128)S(1)} %bitcast.80, bf16[1024,256]{1,0:T(8,128)(2,1)S(1)} %project.5.refs_3_, ...), custom_call_target="tpu_custom_call" | custom-call | flops 9126805504 | bytes 8388608 | tf_op jit(solution)/shard_map/select/pallas_call | solution.py:198
  109.4 3.8 collective-permute-start.21
  113.9 6.1 %collective-permute-done.19 = bf16[2,144,256]{2,1,0:T(8,128)(2,1)S(1)} collective-permute-done((bf16[2,144,256]{2,1,0:T(8,128)(2,1)S(1)}, bf16[2,144,256]{2,1,0:T(8,128)(2,1)S(1)}, u32[]{:S(2)}, u32[]{:S(2)}) %collective-permute-start.19) | collective-permute-done | bytes 147488 | tf_op jit(solution)/shard_map/ppermute | solution.py:34
  121.7 8.0 %collective-permute-done.23.refs_1_ = bf16[8,128,256]{2,1,0:T(8,128)(2,1)S(1)} collective-permute-done((bf16[8,128,256]{2,1,0:T(8,128)(2,1)S(1)}, bf16[8,128,256]{2,1,0:T(8,128)(2,1)S(1)}, u32[]{:S(2)}, u32[]{:S(2)}) %collective-permute-start.23) | collective-permute-done | bytes 524320 | tf_op jit(solution)/shard_map/ppermute | solution.py:29
  132.9 10.0 %collective-permute-done.27.refs_5_ = bf16[8,128,256]{2,1,0:T(8,128)(2,1)S(1)} collective-permute-done((bf16[8,128,256]{2,1,0:T(8,128)(2,1)S(1)}, bf16[8,128,256]{2,1,0:T(8,128)(2,1)S(1)}, u32[]{:S(2)}, u32[]{:S(2)}) %collective-permute-start.27) | collective-permute-done | bytes 524320 | tf_op jit(solution)/shard_map/ppermute | solution.py:29
  156.0 8.1 %panel_gram.1 = (bf16[1024,2048]{1,0:T(8,128)(2,1)}, f32[1024,1024]{1,0:T(8,128)}) custom-call(s32[8]{0:T(128)S(1)} %stack.190.refs_0_.slot, bf16[8,128,256]{2,1,0:T(8,128)(2,1)S(1)} %slice.121.refs_0_, bf16[8,128,256]{2,1,0:T(8,128)(2,1)S(1)} %collective-permute-done.23.refs_1_, bf16[8,128,256]{2,1,0:T(8,128)(2,1)S(1)} %collective-permute-done.24.refs_2_, ...), custom_call_target="tpu_custom_call" | custom-call | flops 4294967296 | bytes 12582912 | tf_op jit(solution)/shard_map/panel_gram/pallas_call | solution.py:234
  164.1 9.0 %collective-permute-start.57 = (f32[1024,1024]{1,0:T(8,128)}, f32[1024,1024]{1,0:T(8,128)}, u32[]{:S(2)}, u32[]{:S(2)}) collective-permute-start(f32[1024,1024]{1,0:T(8,128)} %get-tuple-element.28.g_ref), channel_id=1, source_target_pairs={{0,8},{8,0},{16,24},{24,16},{32,40},{40,32},{48,56},{56,48},{64,72... | collective-permute-start | bytes 12582920 | tf_op jit(solution)/shard_map/ppermute | solution.py:34
  174.9 6.1 %collective-permute-done.32 = bf16[512,256]{1,0:T(8,128)(2,1)S(1)} collective-permute-done((bf16[512,256]{1,0:T(8,128)(2,1)S(1)}, bf16[512,256]{1,0:T(8,128)(2,1)S(1)}, u32[]{:S(2)}, u32[]{:S(2)}) %collective-permute-start.32) | collective-permute-done | bytes 262176 | tf_op jit(solution)/shard_map/ppermute | solution.py:34
  183.9 7.2 %collective-permute-done.33 = bf16[2,128,256]{2,1,0:T(8,128)(2,1)S(1)} collective-permute-done((bf16[2,128,256]{2,1,0:T(8,128)(2,1)S(1)}, bf16[2,128,256]{2,1,0:T(8,128)(2,1)S(1)}, u32[]{:S(2)}, u32[]{:S(2)}) %collective-permute-start.33) | collective-permute-done | bytes 131104 | tf_op jit(solution)/shard_map/ppermute | solution.py:34
  205.5 7.6 %collective-permute-done.39.refs_4_ = bf16[8,128,256]{2,1,0:T(8,128)(2,1)S(1)} collective-permute-done((bf16[8,128,256]{2,1,0:T(8,128)(2,1)S(1)}, bf16[8,128,256]{2,1,0:T(8,128)(2,1)S(1)}, u32[]{:S(2)}, u32[]{:S(2)}) %collective-permute-start.39) | collective-permute-done | bytes 524320 | tf_op jit(solution)/shard_map/ppermute | solution.py:29
  218.0 8.5 %collective-permute-done.47.refs_13_ = bf16[1024,256]{1,0:T(8,128)(2,1)S(1)} collective-permute-done((bf16[1024,256]{1,0:T(8,128)(2,1)S(1)}, bf16[1024,256]{1,0:T(8,128)(2,1)S(1)}, u32[]{:S(2)}, u32[]{:S(2)}) %collective-permute-start.47) | collective-permute-done | bytes 524320 | tf_op jit(solution)/shard_map/ppermute | solution.py:34
  241.8 4.0 collective-permute-done.43.refs_8_
  249.8 21.7 %block_gram.1 = (f32[512,1024]{1,0:T(8,128)}, f32[512,1024]{1,0:T(8,128)}, f32[512,1024]{1,0:T(8,128)}, f32[512,1024]{1,0:T(8,128)}, f32[1024,1024]{1,0:T(8,128)}) custom-call(s32[8]{0:T(128)S(1)} %stack.241.slot, bf16[1024,2048]{1,0:T(8,128)(2,1)} %get-tuple-element.19.pan_ref, bf16[8,128,256]{2,1,0:T(8,128)(2,1)S(1)} %pad_maximum_fusion.refs_0_, ...), custom_call_target="tpu_custom_call" | custom-call | flops 12884901888 | bytes 25165824 | tf_op jit(solution)/shard_map/block_gram/pallas_call | solution.py:280
  271.4 4.2 collective-permute-start.54
  276.4 104.4 %cholesky.1 = (f32[1024,1024]{1,0:T(8,128)S(1)}, f32[1024,128]{1,0:T(8,128)S(1)}) custom-call(f32[1]{0:T(128)} %bitcast.48.count_ref, f32[1024,1024]{1,0:T(8,128)} %get-tuple-element.28.g_ref, f32[1024,1024]{1,0:T(8,128)} %collective-permute-done.57.o_ref), custom_call_target="tpu_custom_call" | custom-call | flops 80000000000 | bytes 12582912 | tf_op jit(solution)/shard_map/cholesky/pallas_call | solution.py:355
  387.1 40.9 %finish.1 = f32[512,1024]{1,0:T(8,128)} custom-call(s32[2]{0:T(128)} %pad_add_fusion.sc, f32[1]{0:T(128)} %bitcast.48.count_ref, f32[512,1024]{1,0:T(8,128)} %get-tuple-element.23.hk_ref, f32[512,1024]{1,0:T(8,128)} %copy-done.31, f32[512,1024]{1,0:T(8,128)} %get-tuple-element.25.pk_ref, f32[512,1024]{1,0:T(8,128)} %copy-done.32, ...), custom_call_target="tpu_custom_call" | custom-call | flops 16000000000 | bytes 29360128 | tf_op jit(solution)/shard_map/finish/pallas_call | solution.py:424
  (220 shorter events, 109.3 us)
Async XLA Ops:
  2.9 15.9 %collective-permute-start.4 = (bf16[272,1024]{1,0:T(8,128)(2,1)S(1)}, bf16[272,1024]{1,0:T(8,128)(2,1)S(1)}, u32[]{:S(2)}, u32[]{:S(2)}) collective-permute-start(bf16[272,1024]{1,0:T(8,128)(2,1)S(1)} %concatenate.35.refs_2_.refs_13_), channel_id=1, source_target_pairs={{0,4},{1,5},{2,6},{3,7},{4,0},{5,1},{6,2},{7,3},{8,12},{9,13},{10,... | collective-permute-start | bytes 1671176 | tf_op jit(solution)/shard_map/ppermute | solution.py:29
  6.7 14.8 %collective-permute-start.2 = (bf16[272,1024]{1,0:T(8,128)(2,1)S(1)}, bf16[272,1024]{1,0:T(8,128)(2,1)S(1)}, u32[]{:S(2)}, u32[]{:S(2)}) collective-permute-start(bf16[272,1024]{1,0:T(8,128)(2,1)S(1)} %concatenate.35.refs_2_.refs_13_), channel_id=1, source_target_pairs={{0,3},{1,0},{2,1},{3,2},{4,7},{5,4},{6,5},{7,6},{8,11},{9,8},{10,9... | collective-permute-start | bytes 1671176 | tf_op jit(solution)/shard_map/ppermute | solution.py:29
  9.2 15.1 %collective-permute-start = (bf16[272,1024]{1,0:T(8,128)(2,1)S(1)}, bf16[272,1024]{1,0:T(8,128)(2,1)S(1)}, u32[]{:S(2)}, u32[]{:S(2)}) collective-permute-start(bf16[272,1024]{1,0:T(8,128)(2,1)S(1)} %concatenate.35.refs_2_.refs_13_), channel_id=1, source_target_pairs={{0,1},{1,2},{2,3},{3,0},{4,5},{5,6},{6,7},{7,4},{8,9},{9,10},{10,1... | collective-permute-start | bytes 1671176 | tf_op jit(solution)/shard_map/ppermute | solution.py:29
  21.3 13.9 %collective-permute-start.5 = (bf16[272,1024]{1,0:T(8,128)(2,1)S(1)}, bf16[272,1024]{1,0:T(8,128)(2,1)S(1)}, u32[]{:S(2)}, u32[]{:S(2)}) collective-permute-start(bf16[272,1024]{1,0:T(8,128)(2,1)S(1)} %collective-permute-done.4.refs_3_.refs_14_), channel_id=1, source_target_pairs={{0,1},{1,2},{2,3},{3,0},{4,5},{5,6},{6,7},{7,4},{8,9},{9,10},{10,1... | collective-permute-start | bytes 1671176 | tf_op jit(solution)/shard_map/ppermute | solution.py:29
  21.5 23.5 %collective-permute-start.3 = (bf16[128,1024]{1,0:T(8,128)(2,1)S(1)}, bf16[128,1024]{1,0:T(8,128)(2,1)S(1)}, u32[]{:S(2)}, u32[]{:S(2)}) collective-permute-start(bf16[128,1024]{1,0:T(8,128)(2,1)S(1)} %slice.113), channel_id=1, source_target_pairs={{0,3},{1,0},{2,1},{3,2},{4,7},{5,4},{6,5},{7,6},{8,11},{9,8},{10,9... | collective-permute-start | bytes 786440 | tf_op jit(solution)/shard_map/ppermute | solution.py:29
  24.3 20.8 %collective-permute-start.1 = (bf16[144,1024]{1,0:T(8,128)(2,1)S(1)}, bf16[144,1024]{1,0:T(8,128)(2,1)S(1)}, u32[]{:S(2)}, u32[]{:S(2)}) collective-permute-start(bf16[144,1024]{1,0:T(8,128)(2,1)S(1)} %slice.112), channel_id=1, source_target_pairs={{0,1},{1,2},{2,3},{3,0},{4,5},{5,6},{6,7},{7,4},{8,9},{9,10},{10,1... | collective-permute-start | bytes 884744 | tf_op jit(solution)/shard_map/ppermute | solution.py:29
  31.7 13.4 %collective-permute-start.8 = (bf16[128,1024]{1,0:T(8,128)(2,1)S(1)}, bf16[128,1024]{1,0:T(8,128)(2,1)S(1)}, u32[]{:S(2)}, u32[]{:S(2)}) collective-permute-start(bf16[128,1024]{1,0:T(8,128)(2,1)S(1)} %slice.115), channel_id=1, source_target_pairs={{0,3},{1,0},{2,1},{3,2},{4,7},{5,4},{6,5},{7,6},{8,11},{9,8},{10,9... | collective-permute-start | bytes 786440 | tf_op jit(solution)/shard_map/ppermute | solution.py:29
  63.7 13.6 %collective-permute-start.13 = (bf16[1024,256]{1,0:T(8,128)(2,1)}, bf16[1024,256]{1,0:T(8,128)(2,1)S(1)}, u32[]{:S(2)}, u32[]{:S(2)}) collective-permute-start(bf16[1024,256]{1,0:T(8,128)(2,1)} %collective-permute-done.9.refs_4_), channel_id=1, source_target_pairs={{0,3},{1,0},{2,1},{3,2},{4,7},{5,4},{6,5},{7,6},{8,11},{9,8},{10,9... | collective-permute-start | bytes 1572872 | tf_op jit(solution)/shard_map/ppermute | solution.py:29
  63.7 16.2 %collective-permute-start.11 = (bf16[1024,256]{1,0:T(8,128)(2,1)}, bf16[1024,256]{1,0:T(8,128)(2,1)S(1)}, u32[]{:S(2)}, u32[]{:S(2)}) collective-permute-start(bf16[1024,256]{1,0:T(8,128)(2,1)} %collective-permute-done.9.refs_4_), channel_id=1, source_target_pairs={{0,1},{1,2},{2,3},{3,0},{4,5},{5,6},{6,7},{7,4},{8,9},{9,10},{10,1... | collective-permute-start | bytes 1572872 | tf_op jit(solution)/shard_map/ppermute | solution.py:29
  66.6 16.3 %collective-permute-start.15 = (bf16[512,256]{1,0:T(8,128)(2,1)}, bf16[512,256]{1,0:T(8,128)(2,1)S(1)}, u32[]{:S(2)}, u32[]{:S(2)}) collective-permute-start(bf16[512,256]{1,0:T(8,128)(2,1)} %slice.117), channel_id=1, source_target_pairs={{0,3},{1,0},{2,1},{3,2},{4,7},{5,4},{6,5},{7,6},{8,11},{9,8},{10,9... | collective-permute-start | bytes 786440 | tf_op jit(solution)/shard_map/ppermute | solution.py:29
  68.6 16.3 %collective-permute-start.14 = (bf16[512,256]{1,0:T(8,128)(2,1)}, bf16[512,256]{1,0:T(8,128)(2,1)}, u32[]{:S(2)}, u32[]{:S(2)}) collective-permute-start(bf16[512,256]{1,0:T(8,128)(2,1)} %slice.116), channel_id=1, source_target_pairs={{0,1},{1,2},{2,3},{3,0},{4,5},{5,6},{6,7},{7,4},{8,9},{9,10},{10,1... | collective-permute-start | bytes 786440 | tf_op jit(solution)/shard_map/ppermute | solution.py:29
  130.0 15.1 %collective-permute-start.25 = (bf16[8,128,256]{2,1,0:T(8,128)(2,1)S(1)}, bf16[8,128,256]{2,1,0:T(8,128)(2,1)S(1)}, u32[]{:S(2)}, u32[]{:S(2)}) collective-permute-start(bf16[8,128,256]{2,1,0:T(8,128)(2,1)S(1)} %collective-permute-done.23.refs_1_), channel_id=1, source_target_pairs={{0,1},{1,2},{2,3},{3,0},{4,5},{5,6},{6,7},{7,4},{8,9},{9,10},{10,1... | collective-permute-start | bytes 1572872 | tf_op jit(solution)/shard_map/ppermute | solution.py:29
  131.2 17.3 %collective-permute-start.29 = (bf16[4,128,256]{2,1,0:T(8,128)(2,1)S(1)}, bf16[4,128,256]{2,1,0:T(8,128)(2,1)S(1)}, u32[]{:S(2)}, u32[]{:S(2)}) collective-permute-start(bf16[4,128,256]{2,1,0:T(8,128)(2,1)S(1)} %slice.123), channel_id=1, source_target_pairs={{0,3},{1,0},{2,1},{3,2},{4,7},{5,4},{6,5},{7,6},{8,11},{9,8},{10,9... | collective-permute-start | bytes 786440 | tf_op jit(solution)/shard_map/ppermute | solution.py:29
  132.8 17.6 %collective-permute-start.28 = (bf16[4,128,256]{2,1,0:T(8,128)(2,1)S(1)}, bf16[4,128,256]{2,1,0:T(8,128)(2,1)S(1)}, u32[]{:S(2)}, u32[]{:S(2)}) collective-permute-start(bf16[4,128,256]{2,1,0:T(8,128)(2,1)S(1)} %slice.122), channel_id=1, source_target_pairs={{0,1},{1,2},{2,3},{3,0},{4,5},{5,6},{6,7},{7,4},{8,9},{9,10},{10,1... | collective-permute-start | bytes 786440 | tf_op jit(solution)/shard_map/ppermute | solution.py:29
  164.1 112.3 %collective-permute-start.57 = (f32[1024,1024]{1,0:T(8,128)}, f32[1024,1024]{1,0:T(8,128)}, u32[]{:S(2)}, u32[]{:S(2)}) collective-permute-start(f32[1024,1024]{1,0:T(8,128)} %get-tuple-element.28.g_ref), channel_id=1, source_target_pairs={{0,8},{8,0},{16,24},{24,16},{32,40},{40,32},{48,56},{56,48},{64,72... | collective-permute-start | bytes 12582920 | tf_op jit(solution)/shard_map/ppermute | solution.py:34
  173.5 26.3 %collective-permute-start.48 = (bf16[1024,256]{1,0:T(8,128)(2,1)S(1)}, bf16[1024,256]{1,0:T(8,128)(2,1)S(1)}, u32[]{:S(2)}, u32[]{:S(2)}) collective-permute-start(bf16[1024,256]{1,0:T(8,128)(2,1)S(1)} %get-tuple-element.22.refs_10_), channel_id=1, source_target_pairs={{0,96},{8,104},{16,112},{24,120},{32,0},{40,8},{48,16},{56,24},{64... | collective-permute-start | bytes 1572872 | tf_op jit(solution)/shard_map/ppermute | solution.py:34
  174.1 26.4 %collective-permute-start.46 = (bf16[1024,256]{1,0:T(8,128)(2,1)S(1)}, bf16[1024,256]{1,0:T(8,128)(2,1)S(1)}, u32[]{:S(2)}, u32[]{:S(2)}) collective-permute-start(bf16[1024,256]{1,0:T(8,128)(2,1)S(1)} %get-tuple-element.22.refs_10_), channel_id=1, source_target_pairs={{0,32},{8,40},{16,48},{24,56},{32,64},{40,72},{48,80},{56,88},{64,... | collective-permute-start | bytes 1572872 | tf_op jit(solution)/shard_map/ppermute | solution.py:34
  199.8 15.6 %collective-permute-start.36 = (bf16[8,128,256]{2,1,0:T(8,128)(2,1)S(1)}, bf16[8,128,256]{2,1,0:T(8,128)(2,1)S(1)}, u32[]{:S(2)}, u32[]{:S(2)}) collective-permute-start(bf16[8,128,256]{2,1,0:T(8,128)(2,1)S(1)} %pad_maximum_fusion.refs_0_), channel_id=1, source_target_pairs={{0,4},{1,5},{2,6},{3,7},{4,0},{5,1},{6,2},{7,3},{8,12},{9,13},{10,... | collective-permute-start | bytes 1572872 | tf_op jit(solution)/shard_map/ppermute | solution.py:29
  200.5 14.9 %collective-permute-start.37 = (bf16[8,128,256]{2,1,0:T(8,128)(2,1)S(1)}, bf16[8,128,256]{2,1,0:T(8,128)(2,1)S(1)}, u32[]{:S(2)}, u32[]{:S(2)}) collective-permute-start(bf16[8,128,256]{2,1,0:T(8,128)(2,1)S(1)} %pad_maximum_fusion.refs_0_), channel_id=1, source_target_pairs={{0,1},{1,2},{2,3},{3,0},{4,5},{5,6},{6,7},{7,4},{8,9},{9,10},{10,1... | collective-permute-start | bytes 1572872 | tf_op jit(solution)/shard_map/ppermute | solution.py:29
  213.0 13.5 %collective-permute-start.47 = (bf16[1024,256]{1,0:T(8,128)(2,1)S(1)}, bf16[1024,256]{1,0:T(8,128)(2,1)S(1)}, u32[]{:S(2)}, u32[]{:S(2)}) collective-permute-start(bf16[1024,256]{1,0:T(8,128)(2,1)S(1)} %collective-permute-done.45.refs_11_), channel_id=1, source_target_pairs={{0,32},{8,40},{16,48},{24,56},{32,64},{40,72},{48,80},{56,88},{64,... | collective-permute-start | bytes 1572872 | tf_op jit(solution)/shard_map/ppermute | solution.py:34
  217.0 14.4 %collective-permute-start.51 = (bf16[512,256]{1,0:T(8,128)(2,1)S(1)}, bf16[512,256]{1,0:T(8,128)(2,1)S(1)}, u32[]{:S(2)}, u32[]{:S(2)}) collective-permute-start(bf16[512,256]{1,0:T(8,128)(2,1)S(1)} %slice.137), channel_id=1, source_target_pairs={{0,96},{8,104},{16,112},{24,120},{32,0},{40,8},{48,16},{56,24},{64... | collective-permute-start | bytes 786440 | tf_op jit(solution)/shard_map/ppermute | solution.py:34
  271.4 112.2 %collective-permute-start.54 = (f32[512,1024]{1,0:T(8,128)}, f32[512,1024]{1,0:T(8,128)S(1)}, u32[]{:S(2)}, u32[]{:S(2)}) collective-permute-start(f32[512,1024]{1,0:T(8,128)} %get-tuple-element.24), channel_id=1, source_target_pairs={{0,8},{8,0},{16,24},{24,16},{32,40},{40,32},{48,56},{56,48},{64,72... | collective-permute-start | bytes 6291464 | tf_op jit(solution)/shard_map/ppermute | solution.py:34
  275.6 108.0 %collective-permute-start.55 = (f32[512,1024]{1,0:T(8,128)}, f32[512,1024]{1,0:T(8,128)S(1)}, u32[]{:S(2)}, u32[]{:S(2)}) collective-permute-start(f32[512,1024]{1,0:T(8,128)} %get-tuple-element.26), channel_id=1, source_target_pairs={{0,8},{8,0},{16,24},{24,16},{32,40},{40,32},{48,56},{56,48},{64,72... | collective-permute-start | bytes 6291464 | tf_op jit(solution)/shard_map/ppermute | solution.py:34
  275.7 107.9 %collective-permute-start.56 = (f32[1024,1024]{1,0:T(8,128)}, f32[1024,1024]{1,0:T(8,128)S(1)}, u32[]{:S(2)}, u32[]{:S(2)}) collective-permute-start(f32[1024,1024]{1,0:T(8,128)} %get-tuple-element.27.pc_ref), channel_id=1, source_target_pairs={{0,8},{8,0},{16,24},{24,16},{32,40},{40,32},{48,56},{56,48},{64,72... | collective-permute-start | bytes 12582920 | tf_op jit(solution)/shard_map/ppermute | solution.py:34
  (68 other events, 902.3 us)
